TPU v7x, 32 devices: a whole 2x2x4 slice. The times are simulated.
32 devices in a mesh: lists: 16 (over z, x, core), sub: 2 (over y).
Axes of the slice: x: 2, y: 2, z: 4, core: 2. Of those that a mesh axis runs over, the one named last changes fastest.
Arguments:
- vectors: bfloat16 [768, 6144], P('sub', 'lists'), may hold values from -6 to 6
- list_ids: int32 [6144], P('lists'), may hold values from 0 to 63
- counts: int32 [16, 16], replicated, may hold values from 0 to 24, as said below
- coarse: bfloat16 [768, 1024], P(None, ('lists', 'sub')), may hold values from -3 to 3
- codebook_init: float32 [768, 256], P('sub'), may hold values from -6 to 6
- codes: int32 [2, 96, 6144], P(None, 'sub', 'lists'), may hold values from 0 to 255
Outputs:
- codebook: float32 [768, 256], P('sub')
- leftover: bfloat16 [768, 6144], P('sub', 'lists')
Inputs may be any that keep to these rules, and one draw needn't show every extreme that they name: `counts`: counts of used slots in each block; in every draw one owner receives full blocks of 24 from every sender. `list_ids`: every slot names one of its block owner's lists.
All inputs are finite; a program needn't handle non-finite values.
Results may differ from a plain program's by a relative error of at most 0.0051.
Values may be sent and summed in bfloat16 or wider, within the bound.
A program may use at most 64 MiB of HBM per device.

v0:
```python
import jax
import jax.numpy as jnp
from jax import lax
from jax.sharding import PartitionSpec as P

K = 256
DS = 8
LISTS_DEV = 64
ITERS = 2


def shards(vectors, list_ids, counts, coarse, codebook_init, codes):
    features, rows = vectors.shape
    owners = lax.axis_size("lists")
    owner = lax.axis_index("lists")
    block = rows // owners
    subspaces = features // DS
    mine = lax.all_to_all(coarse, "sub", split_axis=0, concat_axis=1, tiled=True)
    list_iota = jnp.arange(LISTS_DEV, dtype=jnp.int32)
    arrived = lax.all_to_all(vectors, "lists", split_axis=1, concat_axis=1, tiled=True)
    labels = lax.all_to_all(
        list_ids.reshape(1, rows), "lists", split_axis=1, concat_axis=1, tiled=True
    ).reshape(rows)
    selector = (labels[None, :] == list_iota[:, None]).astype(jnp.bfloat16)
    centre = jnp.dot(mine, selector, preferred_element_type=jnp.float32)
    residual = (arrived.astype(jnp.float32) - centre).astype(jnp.bfloat16)
    block_counts = lax.dynamic_index_in_dim(counts, owner, 1, keepdims=False)
    valid = (jnp.arange(block, dtype=jnp.int32)[None, :] < block_counts[:, None]).reshape(rows)
    code_iota = jnp.arange(K, dtype=jnp.int32)
    split_res = residual.reshape(subspaces, DS, rows)
    group_size = 4
    groups = subspaces // group_size
    grouped_res = split_res.reshape(groups, group_size, DS, rows)
    grouped_codes = jnp.swapaxes(codes, 0, 1).reshape(groups, group_size, ITERS, rows)

    def group_sums(packed):
        sub_res, sub_codes = packed
        one_hot = (sub_codes[:, :, None, :] == code_iota[None, None, :, None]) & valid[
            None, None, None, :
        ]
        one_hot = one_hot.astype(jnp.bfloat16)
        sums = jnp.einsum("gdr,gtkr->tgdk", sub_res, one_hot, preferred_element_type=jnp.float32)
        tally = jnp.swapaxes(jnp.sum(one_hot, axis=3, dtype=jnp.float32), 0, 1)
        return (sums, tally)

    part_sums, part_counts = lax.map(group_sums, (grouped_res, grouped_codes))
    part_sums = jnp.swapaxes(part_sums, 0, 1).reshape(ITERS, features, K)
    part_counts = jnp.swapaxes(part_counts, 0, 1).reshape(ITERS, subspaces, K)
    weight = 0.25 * jnp.sum(counts).astype(jnp.float32) / K
    total_sums, total_counts = lax.psum((part_sums, part_counts), "lists")
    codebook = codebook_init
    for iteration in range(ITERS):
        spread = jnp.repeat(total_counts[iteration], DS, axis=0)
        codebook = (total_sums[iteration] + weight * codebook) / (spread + weight)
    high = codebook.astype(jnp.bfloat16)
    low = (codebook - high.astype(jnp.float32)).astype(jnp.bfloat16)
    books = jnp.concatenate(
        [high.reshape(subspaces, DS, K), low.reshape(subspaces, DS, K)], axis=1
    ).reshape(groups, group_size, 2 * DS, K)

    def group_pick(packed):
        book, sub_codes = packed
        one_hot = (sub_codes[:, None, :] == code_iota[None, :, None]).astype(jnp.bfloat16)
        both = jnp.einsum("gdk,gkr->gdr", book, one_hot, preferred_element_type=jnp.float32)
        return both[:, :DS] + both[:, DS:]

    picked = lax.map(group_pick, (books, grouped_codes[:, :, ITERS - 1]))
    picked = picked.reshape(subspaces, DS, rows)
    leftover = jnp.where(valid[None, None, :], split_res.astype(jnp.float32) - picked, 0.0)
    leftover = leftover.astype(jnp.bfloat16).reshape(features, rows)
    return (codebook, leftover)


def solution(mesh):
    return jax.shard_map(
        shards,
        mesh=mesh,
        in_specs=(
            P("sub", "lists"),
            P("lists"),
            P(),
            P(None, ("lists", "sub")),
            P("sub", None),
            P(None, "sub", "lists"),
        ),
        out_specs=(P("sub", None), P("sub", "lists")),
        check_vma=False,
    )
```

profile of v0, /device:TPU:0, one launch (start us, length us, event | category | flops | bytes accessed | tf_op | source)
XLA Modules:
  0.0 176.7 jit_solution(4619838477152994786)
XLA Ops:
  7.2 1.4 all_to_all.28
  8.6 7.4 %all-to-all-start.1 = ((s32[1,16,24]{2,0,1:T(1,128)}), s32[1,16,24]{2,0,1:T(1,128)S(1)}, u32[]{:S(2)}, u32[]{:S(2)}) async-start(s32[1,16,24]{2,0,1:T(1,128)} %all_to_all.28), calls=%async_computation.1 | async-start | bytes 16384 | tf_op jit(solution)/shard_map/all_to_all | solution.py:21
  16.0 1.9 %copy.21 = bf16[384,384]{0,1:T(8,128)(2,1)} copy(bf16[384,384]{1,0:T(8,128)(2,1)} %param.10) | data formatting | bytes 589824 | tf_op args[0]
  17.8 4.5 %all-to-all-done.1 = s32[1,16,24]{2,0,1:T(1,128)S(1)} async-done(((s32[1,16,24]{2,0,1:T(1,128)}), s32[1,16,24]{2,0,1:T(1,128)S(1)}, u32[]{:S(2)}, u32[]{:S(2)}) %all-to-all-start.1) | async-done | bytes 1568 | tf_op jit(solution)/shard_map/all_to_all | solution.py:21
  22.3 3.5 %all-to-all-start = ((bf16[384,16,24]{0,2,1:T(8,128)(2,1)}), bf16[384,16,24]{0,2,1:T(8,128)(2,1)S(1)}, u32[]{:S(2)}, u32[]{:S(2)}) async-start(bf16[384,16,24]{0,2,1:T(8,128)(2,1)} %bitcast.1), calls=%async_computation | async-start | bytes 589824 | tf_op jit(solution)/shard_map/all_to_all | solution.py:20
  25.9 0.6 copy.36
  26.6 0.7 reduce_sum.18
  28.6 0.6 reduce.5
  29.4 7.0 %all-to-all-done = bf16[384,16,24]{0,2,1:T(8,128)(2,1)S(1)} async-done(((bf16[384,16,24]{0,2,1:T(8,128)(2,1)}), bf16[384,16,24]{0,2,1:T(8,128)(2,1)S(1)}, u32[]{:S(2)}, u32[]{:S(2)}) %all-to-all-start) | async-done | bytes 294944 | tf_op jit(solution)/shard_map/all_to_all | solution.py:20
  36.4 3.3 %all-to-all-start.2 = ((bf16[2,384,32]{1,2,0:T(8,128)(2,1)}), bf16[2,384,32]{1,2,0:T(8,128)(2,1)S(1)}, u32[]{:S(2)}, u32[]{:S(2)}) async-start(bf16[2,384,32]{1,2,0:T(8,128)(2,1)} %bitcast.93), calls=%async_computation.2 | async-start | bytes 98304 | tf_op jit(solution)/shard_map/all_to_all | solution.py:18
  40.0 3.7 %all-to-all-done.2 = bf16[2,384,32]{1,2,0:T(8,128)(2,1)S(1)} async-done(((bf16[2,384,32]{1,2,0:T(8,128)(2,1)}), bf16[2,384,32]{1,2,0:T(8,128)(2,1)S(1)}, u32[]{:S(2)}, u32[]{:S(2)}) %all-to-all-start.2) | async-done | bytes 49184 | tf_op jit(solution)/shard_map/all_to_all | solution.py:18
  44.0 25.4 %while.24 = (s32[]{:T(128)}, f32[12,2,4,8,256]{4,3,1,2,0:T(8,128)S(1)}, f32[12,2,4,256]{3,1,2,0:T(2,128)}, s32[12,4,2,384]{3,1,0,2:T(4,128)S(1)}, bf16[12,4,8,38...) while((s32[]{:T(128)}, f32[12,2,4,8,256]{4,3,1,2,0:T(8,128)S(1)}, ...), condition=%wide.region_2.3_spmd.clone, body=%wide.region_0.2_spmd.clone.sunk | while | flops 18086272 | bytes 192145 | solution.py:46
  44.2 0.7 fusion.48
  44.9 0.6 convert_reduce_fusion.2
  45.5 0.6 bitcast_dynamic-update-slice_fusion.2
  46.3 0.7 fusion.48
  47.0 0.6 convert_reduce_fusion.2
  47.6 0.6 bitcast_dynamic-update-slice_fusion.2
  48.4 0.7 fusion.48
  49.1 0.6 convert_reduce_fusion.2
  50.5 0.7 fusion.48
  51.2 0.6 convert_reduce_fusion.2
  52.6 0.7 fusion.48
  53.3 0.6 convert_reduce_fusion.2
  54.0 0.6 bitcast_dynamic-update-slice_fusion.2
  54.8 0.7 fusion.48
  55.4 0.6 convert_reduce_fusion.2
  56.1 0.6 bitcast_dynamic-update-slice_fusion.2
  56.9 0.7 fusion.48
  57.6 0.6 convert_reduce_fusion.2
  59.0 0.7 fusion.48
  59.7 0.6 convert_reduce_fusion.2
  61.1 0.7 fusion.48
  61.8 0.6 convert_reduce_fusion.2
  62.4 0.6 bitcast_dynamic-update-slice_fusion.2
  63.2 0.7 fusion.48
  63.9 0.6 convert_reduce_fusion.2
  64.5 0.6 bitcast_dynamic-update-slice_fusion.2
  65.3 0.7 fusion.48
  66.0 0.6 convert_reduce_fusion.2
  67.4 0.7 fusion.48
  68.1 0.6 convert_reduce_fusion.2
  69.4 1.0 copy.25
  70.6 90.5 %all-reduce.3.cloned.1.call-done = (f32[2,384,256]{2,1,0:T(8,128)}, f32[2,48,256]{2,0,1:T(2,128)}) async-done(((f32[2,384,256]{2,1,0:T(8,128)}, f32[2,48,256]{2,0,1:T(2,128)}), (f32[2,384,256]{2,1,0:T(8,128)}, f32[2,48,256]{2,0,1:T(2,128)})) %all-reduce.3.cloned.1.call-update) | async-done | bytes 884752 | tf_op jit(solution)/shard_map/psum | solution.py:50
  161.1 1.1 slice_add_fusion.2
  162.2 2.0 %subtract_convert_fusion = (bf16[384,256]{1,0:T(8,128)(2,1)S(1)}, bf16[384,256]{1,0:T(8,128)(2,1)S(1)}, f32[384,256]{1,0:T(8,128)}) fusion(f32[48,256]{1,0:T(8,128)S(1)} %get-tuple-element.147, f32[48,256]{1,0:T(8,128)S(1)} %get-tuple-element.148, f32[384,256]{1,0:T(8,128)S(1)} %copy-done, f32[2,384,256]{2,1,0:T(8,128)} %get-tuple-element.140, f32[]{:T(128)S(6)} %div.9), kind=kLoop, calls=%fused_computation.43 | loop fusion | flops 983040 | bytes 2064388 | tf_op jit(solution)/shard_map/convert_element_type | solution.py:56
  164.2 4.8 %while.25 = (s32[]{:T(128)}, f32[12,4,8,384]{3,2,1,0:T(8,128)S(1)}, bf16[12,4,16,256]{3,2,1,0:T(8,128)(2,1)S(1)}, s32[12,4,384]{2,1,0:T(4,128)S(1)}, s32[]{:T(128)}) while((s32[]{:T(128)}, f32[12,4,8,384]{3,2,1,0:T(8,128)S(1)}, bf16[12,4,16,256]{3,2,1,0:T(8,128)(2,1)S(1)}, s32[12,4,384]{2,1,0:T(4,128)S(1)}, s32[]{:T(128)}) %tuple.52), condition=%wide.region_7.8_spmd.clone, body=%wide.region_6.7_spmd.clone.sunk | while | flops 12988418 | bytes 297033 | solution.py:67
  169.0 0.8 fusion.31
  (115 shorter events, 12.1 us)
Async XLA Ops:
  7.2 18.7 %copy-start.2 = (bf16[768,32]{0,1:T(8,128)(2,1)S(1)}, bf16[768,32]{0,1:T(8,128)(2,1)}, u32[]{:S(2)}) copy-start(bf16[768,32]{0,1:T(8,128)(2,1)} %param.13) | copy-start | bytes 147460
  7.2 19.3 %copy-start.1 = (s32[2,48,384]{2,1,0:T(8,128)S(1)}, s32[2,48,384]{2,1,0:T(8,128)}, u32[]{:S(2)}) copy-start(s32[2,48,384]{2,1,0:T(8,128)} %param.15) | copy-start | bytes 442372
  8.6 13.7 %all-to-all-start.1 = ((s32[1,16,24]{2,0,1:T(1,128)}), s32[1,16,24]{2,0,1:T(1,128)S(1)}, u32[]{:S(2)}, u32[]{:S(2)}) async-start(s32[1,16,24]{2,0,1:T(1,128)} %all_to_all.28), calls=%async_computation.1 | async-start | bytes 16384 | tf_op jit(solution)/shard_map/all_to_all | solution.py:21
  16.0 10.6 %copy-start.3 = (s32[16,16]{1,0:T(8,128)S(1)}, s32[16,16]{1,0:T(8,128)}, u32[]{:S(2)}) copy-start(s32[16,16]{1,0:T(8,128)} %param.12) | copy-start | bytes 3076
  22.3 14.1 %all-to-all-start = ((bf16[384,16,24]{0,2,1:T(8,128)(2,1)}), bf16[384,16,24]{0,2,1:T(8,128)(2,1)S(1)}, u32[]{:S(2)}, u32[]{:S(2)}) async-start(bf16[384,16,24]{0,2,1:T(8,128)(2,1)} %bitcast.1), calls=%async_computation | async-start | bytes 589824 | tf_op jit(solution)/shard_map/all_to_all | solution.py:20
  36.4 7.3 %all-to-all-start.2 = ((bf16[2,384,32]{1,2,0:T(8,128)(2,1)}), bf16[2,384,32]{1,2,0:T(8,128)(2,1)S(1)}, u32[]{:S(2)}, u32[]{:S(2)}) async-start(bf16[2,384,32]{1,2,0:T(8,128)(2,1)} %bitcast.93), calls=%async_computation.2 | async-start | bytes 98304 | tf_op jit(solution)/shard_map/all_to_all | solution.py:18
  39.7 121.4 %all-reduce.3.cloned.1.call-start = ((), (), s32[]{:S(2)}) async-start(), calls=%async_computation.3 | async-start | bytes 1769472 | tf_op jit(solution)/shard_map/psum | solution.py:50
  70.3 91.8 %copy-start = (f32[384,256]{1,0:T(8,128)S(1)}, f32[384,256]{1,0:T(8,128)}, u32[]{:S(2)}) copy-start(f32[384,256]{1,0:T(8,128)} %param.14) | copy-start | bytes 1179652
Sparse Core Ops, SparseCore 0:
  70.5 90.5 all-reduce.2
where the time goes:
time: 177 us
  waiting for transfers between devices  106 us (60%)
  local copies, waits for them, and re-layouts  14.8 us (8%)
  between operations  14.8 us (8%)
  starting transfers between devices  14.2 us (8%)
  other arithmetic  13.8 us (8%)
  matrix products  12.8 us (7%)
    psum x1, waiting for transfers between devices, shards(): total_sums, total_counts = lax.psum((part_sums, part_counts), 'lists')  90.5 us
    dot_general x12, matrix products, group_sums(): jnp.einsum('gdr,gtkr->tgdk', sub_res, one_hot, preferred_element_type=jnp...  8.24 us
    reduce_sum x12, other arithmetic, group_sums(): tally = jnp.swapaxes(jnp.sum(one_hot, axis=3, dtype=jnp.float32), 0, 1)  7.52 us
    all_to_all x1, starting transfers between devices, shards(): lax.all_to_all(list_ids.reshape(1, rows), 'lists', split_axis=1, concat_a...  7.36 us
    dynamic_update_slice x12, local copies, waits for them, and re-layouts, shards(): part_sums, part_counts = lax.map(group_sums, (grouped_res, grouped_codes))  7.27 us
    all_to_all x1, waiting for transfers between devices, shards(): lax.all_to_all(vectors, 'lists', split_axis=1, concat_axis=1, tiled=True)  7 us
    all_to_all x1, waiting for transfers between devices, shards(): lax.all_to_all(list_ids.reshape(1, rows), 'lists', split_axis=1, concat_a...  4.47 us
    dot_general x12, matrix products, group_pick(): jnp.einsum('gdk,gkr->gdr', book, one_hot, preferred_element_type=jnp.floa...  4.29 us
  transfers between devices with their start and end apart: 4, of which 4 were waited for; matrix products, arithmetic and copies ran while one was open for 3% of the time, Pallas kernels for 0%

commit v1 on v0

--- a/solution.py
+++ b/solution.py
@@ -9,6 +9,29 @@
 ITERS = 2
 
 
+def split_up(value, dim, size):
+    lengths = value.shape
+    blocks = value.reshape(*lengths[:dim], size, lengths[dim] // size, *lengths[dim + 1 :])
+    return jnp.moveaxis(blocks, dim, 0)
+
+
+def laid_out(parts, dim):
+    shape = list(parts.shape[1:])
+    shape[dim] *= parts.shape[0]
+    return jnp.moveaxis(parts, 0, dim).reshape(shape)
+
+
+def exchange_in_pairs(x, axis, split_dim, concat_dim):
+    length, mine = (lax.axis_size(axis), lax.axis_index(axis))
+    parts = split_up(x, split_dim, length)
+    outs = [parts[mine]]
+    for step in range(1, length):
+        sent = parts[mine ^ step]
+        outs.append(lax.ppermute(sent, axis, [(i, i ^ step) for i in range(length)]))
+    parts = jnp.stack(outs)[mine ^ jnp.arange(length)]
+    return laid_out(parts, concat_dim)
+
+
 def shards(vectors, list_ids, counts, coarse, codebook_init, codes):
     features, rows = vectors.shape
     owners = lax.axis_size("lists")
@@ -17,7 +40,7 @@
     subspaces = features // DS
     mine = lax.all_to_all(coarse, "sub", split_axis=0, concat_axis=1, tiled=True)
     list_iota = jnp.arange(LISTS_DEV, dtype=jnp.int32)
-    arrived = lax.all_to_all(vectors, "lists", split_axis=1, concat_axis=1, tiled=True)
+    arrived = exchange_in_pairs(vectors, "lists", 1, 1)
     labels = lax.all_to_all(
         list_ids.reshape(1, rows), "lists", split_axis=1, concat_axis=1, tiled=True
     ).reshape(rows)

time: 177 us -> 189 us (1.068)
  starting transfers between devices: 14.2 us -> 31.1 us
  waiting for transfers between devices: 106 us -> 101 us
    ppermute x0 -> x15, starting transfers between devices: none -> 21.8 us  [exchange_in_pairs(): lax.ppermute(sent, axis, [(i, i ^ step) for i in range(length)])]
    all_to_all x1 -> x0, waiting for transfers between devices: 7 us -> none  [shards(): lax.all_to_all(vectors, 'lists', split_axis=1, concat_axis=1, tiled=True)]
    all_to_all x1, waiting for transfers between devices: 3.66 us -> 0.01 us  [shards(): lax.all_to_all(coarse, 'sub', split_axis=0, concat_axis=1, tiled=True)]
    psum x1, waiting for transfers between devices: 90.5 us -> 94.1 us  [shards(): total_sums, total_counts = lax.psum((part_sums, part_counts), 'lists')]
    all_to_all x1 -> x0, starting transfers between devices: 3.54 us -> none  [shards(): lax.all_to_all(vectors, 'lists', split_axis=1, concat_axis=1, tiled=True)]
    ppermute x0 -> x15, waiting for transfers between devices: none -> 2.8 us  [exchange_in_pairs(): lax.ppermute(sent, axis, [(i, i ^ step) for i in range(length)])]
  transfers between devices with their start and end apart: 4 -> 18, of which waited for: 4 -> 4; matrix products, arithmetic and copies ran while one was open for 3% -> 2% of each run, Pallas kernels for 0% -> 0%
where the time goes in v1:
time: 189 us
  waiting for transfers between devices  101 us (53%)
  starting transfers between devices  31.1 us (16%)
  between operations  15.1 us (8%)
  local copies, waits for them, and re-layouts  14.3 us (8%)
  other arithmetic  13.7 us (7%)
  matrix products  12.8 us (7%)
    psum x1, waiting for transfers between devices, shards(): total_sums, total_counts = lax.psum((part_sums, part_counts), 'lists')  94.1 us
    ppermute x15, starting transfers between devices, exchange_in_pairs(): lax.ppermute(sent, axis, [(i, i ^ step) for i in range(length)])  21.8 us
    dot_general x12, matrix products, group_sums(): jnp.einsum('gdr,gtkr->tgdk', sub_res, one_hot, preferred_element_type=jnp...  8.24 us
    reduce_sum x12, other arithmetic, group_sums(): tally = jnp.swapaxes(jnp.sum(one_hot, axis=3, dtype=jnp.float32), 0, 1)  7.52 us
    dynamic_update_slice x12, local copies, waits for them, and re-layouts, shards(): part_sums, part_counts = lax.map(group_sums, (grouped_res, grouped_codes))  7.27 us
    all_to_all x1, starting transfers between devices, shards(): lax.all_to_all(list_ids.reshape(1, rows), 'lists', split_axis=1, concat_a...  6.06 us
    dot_general x12, matrix products, group_pick(): jnp.einsum('gdk,gkr->gdr', book, one_hot, preferred_element_type=jnp.floa...  4.29 us
    all_to_all x1, waiting for transfers between devices, shards(): lax.all_to_all(list_ids.reshape(1, rows), 'lists', split_axis=1, concat_a...  4.14 us
  transfers between devices with their start and end apart: 18, of which 4 were waited for; matrix products, arithmetic and copies ran while one was open for 2% of the time, Pallas kernels for 0%

profile of v1, /device:TPU:0, one launch (start us, length us, event | category | flops | bytes accessed | tf_op | source)
XLA Modules:
  0.0 188.6 jit_solution(4987520160186209619)
XLA Ops:
  7.3 1.2 copy.21
  9.2 2.6 %collective-permute-start.1 = (bf16[384,24]{0,1:T(8,128)(2,1)S(1)}, bf16[384,24]{0,1:T(8,128)(2,1)S(1)}, u32[]{:S(2)}, u32[]{:S(2)}) collective-permute-start(bf16[384,24]{0,1:T(8,128)(2,1)S(1)} %get-tuple-element.158), channel_id=1, source_target_pairs={{0,4},{2,6},{4,0},{6,2},{8,12},{10,14},{12,8},{14,10},{16,20},{18,... | collective-permute-start | bytes 55304 | tf_op jit(solution)/shard_map/ppermute | solution.py:30
  11.8 1.8 collective-permute-start.3
  13.6 0.7 all_to_all.20
  14.3 6.1 %all-to-all-start = ((s32[1,16,24]{2,0,1:T(1,128)}), s32[1,16,24]{2,0,1:T(1,128)S(1)}, u32[]{:S(2)}, u32[]{:S(2)}) async-start(s32[1,16,24]{2,0,1:T(1,128)} %all_to_all.20), calls=%async_computation | async-start | bytes 16384 | tf_op jit(solution)/shard_map/all_to_all | solution.py:44
  21.2 0.7 reduce_sum.18
  22.6 4.1 %all-to-all-done = s32[1,16,24]{2,0,1:T(1,128)S(1)} async-done(((s32[1,16,24]{2,0,1:T(1,128)}), s32[1,16,24]{2,0,1:T(1,128)S(1)}, u32[]{:S(2)}, u32[]{:S(2)}) %all-to-all-start) | async-done | bytes 1568 | tf_op jit(solution)/shard_map/all_to_all | solution.py:44
  26.8 3.3 %all-to-all-start.1 = ((bf16[2,384,32]{1,2,0:T(8,128)(2,1)}), bf16[2,384,32]{1,2,0:T(8,128)(2,1)S(1)}, u32[]{:S(2)}, u32[]{:S(2)}) async-start(bf16[2,384,32]{1,2,0:T(8,128)(2,1)} %bitcast.157), calls=%async_computation.1 | async-start | bytes 98304 | tf_op jit(solution)/shard_map/all_to_all | solution.py:41
  31.9 1.6 collective-permute-start.6
  33.5 0.6 collective-permute-start.7
  34.2 2.7 %collective-permute-start.8 = (bf16[384,24]{0,1:T(8,128)(2,1)S(1)}, bf16[384,24]{0,1:T(8,128)(2,1)S(1)}, u32[]{:S(2)}, u32[]{:S(2)}) collective-permute-start(bf16[384,24]{0,1:T(8,128)(2,1)S(1)} %get-tuple-element.151), channel_id=1, source_target_pairs={{0,18},{2,16},{4,22},{6,20},{8,26},{10,24},{12,30},{14,28},{16,2},... | collective-permute-start | bytes 55304 | tf_op jit(solution)/shard_map/ppermute | solution.py:30
  37.5 2.5 %collective-permute-start.10 = (bf16[384,24]{0,1:T(8,128)(2,1)S(1)}, bf16[384,24]{0,1:T(8,128)(2,1)S(1)}, u32[]{:S(2)}, u32[]{:S(2)}) collective-permute-start(bf16[384,24]{0,1:T(8,128)(2,1)S(1)} %get-tuple-element.149), channel_id=1, source_target_pairs={{0,22},{2,20},{4,18},{6,16},{8,30},{10,28},{12,26},{14,24},{16,6},... | collective-permute-start | bytes 55304 | tf_op jit(solution)/shard_map/ppermute | solution.py:30
  40.0 0.7 collective-permute-start.11
  40.7 3.6 %collective-permute-start.12 = (bf16[384,24]{0,1:T(8,128)(2,1)S(1)}, bf16[384,24]{0,1:T(8,128)(2,1)S(1)}, u32[]{:S(2)}, u32[]{:S(2)}) collective-permute-start(bf16[384,24]{0,1:T(8,128)(2,1)S(1)} %get-tuple-element.147), channel_id=1, source_target_pairs={{0,26},{2,24},{4,30},{6,28},{8,18},{10,16},{12,22},{14,20},{16,10}... | collective-permute-start | bytes 55304 | tf_op jit(solution)/shard_map/ppermute | solution.py:30
  44.3 0.7 collective-permute-start.13
  44.9 3.3 %collective-permute-start.14 = (bf16[384,24]{0,1:T(8,128)(2,1)S(1)}, bf16[384,24]{0,1:T(8,128)(2,1)S(1)}, u32[]{:S(2)}, u32[]{:S(2)}) collective-permute-start(bf16[384,24]{0,1:T(8,128)(2,1)S(1)} %get-tuple-element.145), channel_id=1, source_target_pairs={{0,30},{2,28},{4,26},{6,24},{8,22},{10,20},{12,18},{14,16},{16,14}... | collective-permute-start | bytes 55304 | tf_op jit(solution)/shard_map/ppermute | solution.py:30
  48.3 2.6 %collective-permute-done.13 = bf16[384,24]{0,1:T(8,128)(2,1)S(1)} collective-permute-done((bf16[384,24]{0,1:T(8,128)(2,1)S(1)}, bf16[384,24]{0,1:T(8,128)(2,1)S(1)}, u32[]{:S(2)}, u32[]{:S(2)}) %collective-permute-start.13) | collective-permute-done | bytes 18464 | tf_op jit(solution)/shard_map/ppermute | solution.py:30
  52.3 25.4 %while.24 = (s32[]{:T(128)}, f32[12,2,4,8,256]{4,3,1,2,0:T(8,128)S(1)}, f32[12,2,4,256]{3,1,2,0:T(2,128)}, s32[12,4,2,384]{3,1,0,2:T(4,128)S(1)}, bf16[12,4,8,38...) while((s32[]{:T(128)}, f32[12,2,4,8,256]{4,3,1,2,0:T(8,128)S(1)}, ...), condition=%wide.region_2.3_spmd.clone, body=%wide.region_0.2_spmd.clone.sunk | while | flops 18086272 | bytes 192145 | solution.py:69
  52.5 0.7 fusion.49
  53.2 0.6 convert_reduce_fusion.2
  54.6 0.7 fusion.49
  55.3 0.6 convert_reduce_fusion.2
  56.7 0.7 fusion.49
  57.4 0.6 convert_reduce_fusion.2
  58.8 0.7 fusion.49
  59.5 0.6 convert_reduce_fusion.2
  60.9 0.7 fusion.49
  61.6 0.6 convert_reduce_fusion.2
  63.0 0.7 fusion.49
  63.7 0.6 convert_reduce_fusion.2
  65.2 0.7 fusion.49
  65.8 0.6 convert_reduce_fusion.2
  67.3 0.7 fusion.49
  68.0 0.6 convert_reduce_fusion.2
  69.4 0.7 fusion.49
  70.1 0.6 convert_reduce_fusion.2
  71.5 0.7 fusion.49
  72.2 0.6 convert_reduce_fusion.2
  73.6 0.7 fusion.49
  74.3 0.6 convert_reduce_fusion.2
  75.7 0.7 fusion.49
  76.4 0.6 convert_reduce_fusion.2
  77.6 1.0 copy.25
  78.9 94.1 %all-reduce.3.cloned.1.call-done = (f32[2,384,256]{2,1,0:T(8,128)}, f32[2,48,256]{2,0,1:T(2,128)}) async-done(((f32[2,384,256]{2,1,0:T(8,128)}, f32[2,48,256]{2,0,1:T(2,128)}), (f32[2,384,256]{2,1,0:T(8,128)}, f32[2,48,256]{2,0,1:T(2,128)})) %all-reduce.3.cloned.1.call-update) | async-done | bytes 884752 | tf_op jit(solution)/shard_map/psum | solution.py:73
  173.0 1.1 slice_add_fusion.2
  174.1 2.0 %subtract_convert_fusion = (bf16[384,256]{1,0:T(8,128)(2,1)S(1)}, bf16[384,256]{1,0:T(8,128)(2,1)S(1)}, f32[384,256]{1,0:T(8,128)}) fusion(f32[48,256]{1,0:T(8,128)S(1)} %get-tuple-element.162, f32[48,256]{1,0:T(8,128)S(1)} %get-tuple-element.163, f32[384,256]{1,0:T(8,128)S(1)} %copy-done, f32[2,384,256]{2,1,0:T(8,128)} %get-tuple-element.140, f32[]{:T(128)S(6)} %div.9), kind=kLoop, calls=%fused_computation.44 | loop fusion | flops 983040 | bytes 2064388 | tf_op jit(solution)/shard_map/convert_element_type | solution.py:79
  176.1 4.8 %while.25 = (s32[]{:T(128)}, f32[12,4,8,384]{3,2,1,0:T(8,128)S(1)}, bf16[12,4,16,256]{3,2,1,0:T(8,128)(2,1)S(1)}, s32[12,4,384]{2,1,0:T(4,128)S(1)}, s32[]{:T(128)}) while((s32[]{:T(128)}, f32[12,4,8,384]{3,2,1,0:T(8,128)S(1)}, bf16[12,4,16,256]{3,2,1,0:T(8,128)(2,1)S(1)}, s32[12,4,384]{2,1,0:T(4,128)S(1)}, s32[]{:T(128)}) %tuple.66), condition=%wide.region_7.8_spmd.clone, body=%wide.region_6.7_spmd.clone.sunk | while | flops 12988418 | bytes 297033 | solution.py:90
  180.9 0.8 fusion.31
  (165 shorter events, 19.7 us)
Async XLA Ops:
  7.2 6.5 %copy-start.4 = (s32[384]{0:T(512)S(1)}, s32[384]{0:T(512)}, u32[]{:S(2)}) copy-start(s32[384]{0:T(512)} %param.11) | copy-start | bytes 4612
  7.2 13.3 %copy-start.2 = (bf16[768,32]{0,1:T(8,128)(2,1)S(1)}, bf16[768,32]{0,1:T(8,128)(2,1)}, u32[]{:S(2)}) copy-start(bf16[768,32]{0,1:T(8,128)(2,1)} %param.13) | copy-start | bytes 147460
  7.2 13.9 %copy-start.1 = (s32[2,48,384]{2,1,0:T(8,128)S(1)}, s32[2,48,384]{2,1,0:T(8,128)}, u32[]{:S(2)}) copy-start(s32[2,48,384]{2,1,0:T(8,128)} %param.15) | copy-start | bytes 442372
  7.3 13.9 %copy-start.3 = (s32[16,16]{1,0:T(8,128)S(1)}, s32[16,16]{1,0:T(8,128)}, u32[]{:S(2)}) copy-start(s32[16,16]{1,0:T(8,128)} %param.12) | copy-start | bytes 3076
  8.6 22.7 %collective-permute-start = (bf16[384,24]{0,1:T(8,128)(2,1)S(1)}, bf16[384,24]{0,1:T(8,128)(2,1)S(1)}, u32[]{:S(2)}, u32[]{:S(2)}) collective-permute-start(bf16[384,24]{0,1:T(8,128)(2,1)S(1)} %get-tuple-element.159), channel_id=1, source_target_pairs={{0,2},{2,0},{4,6},{6,4},{8,10},{10,8},{12,14},{14,12},{16,18},{18,... | collective-permute-start | bytes 55304 | tf_op jit(solution)/shard_map/ppermute | solution.py:30
  9.2 22.8 %collective-permute-start.1 = (bf16[384,24]{0,1:T(8,128)(2,1)S(1)}, bf16[384,24]{0,1:T(8,128)(2,1)S(1)}, u32[]{:S(2)}, u32[]{:S(2)}) collective-permute-start(bf16[384,24]{0,1:T(8,128)(2,1)S(1)} %get-tuple-element.158), channel_id=1, source_target_pairs={{0,4},{2,6},{4,0},{6,2},{8,12},{10,14},{12,8},{14,10},{16,20},{18,... | collective-permute-start | bytes 55304 | tf_op jit(solution)/shard_map/ppermute | solution.py:30
  11.7 21.8 %collective-permute-start.2 = (bf16[384,24]{0,1:T(8,128)(2,1)S(1)}, bf16[384,24]{0,1:T(8,128)(2,1)S(1)}, u32[]{:S(2)}, u32[]{:S(2)}) collective-permute-start(bf16[384,24]{0,1:T(8,128)(2,1)S(1)} %get-tuple-element.157), channel_id=1, source_target_pairs={{0,6},{2,4},{4,2},{6,0},{8,14},{10,12},{12,10},{14,8},{16,22},{18,... | collective-permute-start | bytes 55304 | tf_op jit(solution)/shard_map/ppermute | solution.py:30
  11.8 22.4 %collective-permute-start.3 = (bf16[384,24]{0,1:T(8,128)(2,1)S(1)}, bf16[384,24]{0,1:T(8,128)(2,1)S(1)}, u32[]{:S(2)}, u32[]{:S(2)}) collective-permute-start(bf16[384,24]{0,1:T(8,128)(2,1)S(1)} %get-tuple-element.156), channel_id=1, source_target_pairs={{0,8},{2,10},{4,12},{6,14},{8,0},{10,2},{12,4},{14,6},{16,24},{18,... | collective-permute-start | bytes 55304 | tf_op jit(solution)/shard_map/ppermute | solution.py:30
  13.6 23.3 %collective-permute-start.4 = (bf16[384,24]{0,1:T(8,128)(2,1)S(1)}, bf16[384,24]{0,1:T(8,128)(2,1)S(1)}, u32[]{:S(2)}, u32[]{:S(2)}) collective-permute-start(bf16[384,24]{0,1:T(8,128)(2,1)S(1)} %get-tuple-element.155), channel_id=1, source_target_pairs={{0,10},{2,8},{4,14},{6,12},{8,2},{10,0},{12,6},{14,4},{16,26},{18,... | collective-permute-start | bytes 55304 | tf_op jit(solution)/shard_map/ppermute | solution.py:30
  14.3 12.5 %all-to-all-start = ((s32[1,16,24]{2,0,1:T(1,128)}), s32[1,16,24]{2,0,1:T(1,128)S(1)}, u32[]{:S(2)}, u32[]{:S(2)}) async-start(s32[1,16,24]{2,0,1:T(1,128)} %all_to_all.20), calls=%async_computation | async-start | bytes 16384 | tf_op jit(solution)/shard_map/all_to_all | solution.py:44
  26.8 25.2 %all-to-all-start.1 = ((bf16[2,384,32]{1,2,0:T(8,128)(2,1)}), bf16[2,384,32]{1,2,0:T(8,128)(2,1)S(1)}, u32[]{:S(2)}, u32[]{:S(2)}) async-start(bf16[2,384,32]{1,2,0:T(8,128)(2,1)} %bitcast.157), calls=%async_computation.1 | async-start | bytes 98304 | tf_op jit(solution)/shard_map/all_to_all | solution.py:41
  30.1 142.9 %all-reduce.3.cloned.1.call-start = ((), (), s32[]{:S(2)}) async-start(), calls=%async_computation.2 | async-start | bytes 1769472 | tf_op jit(solution)/shard_map/psum | solution.py:73
  31.3 6.2 %collective-permute-start.5 = (bf16[384,24]{0,1:T(8,128)(2,1)S(1)}, bf16[384,24]{0,1:T(8,128)(2,1)S(1)}, u32[]{:S(2)}, u32[]{:S(2)}) collective-permute-start(bf16[384,24]{0,1:T(8,128)(2,1)S(1)} %get-tuple-element.154), channel_id=1, source_target_pairs={{0,12},{2,14},{4,8},{6,10},{8,4},{10,6},{12,0},{14,2},{16,28},{18,... | collective-permute-start | bytes 55304 | tf_op jit(solution)/shard_map/ppermute | solution.py:30
  31.9 8.0 %collective-permute-start.6 = (bf16[384,24]{0,1:T(8,128)(2,1)S(1)}, bf16[384,24]{0,1:T(8,128)(2,1)S(1)}, u32[]{:S(2)}, u32[]{:S(2)}) collective-permute-start(bf16[384,24]{0,1:T(8,128)(2,1)S(1)} %get-tuple-element.153), channel_id=1, source_target_pairs={{0,14},{2,12},{4,10},{6,8},{8,6},{10,4},{12,2},{14,0},{16,30},{18,... | collective-permute-start | bytes 55304 | tf_op jit(solution)/shard_map/ppermute | solution.py:30
  33.5 7.2 %collective-permute-start.7 = (bf16[384,24]{0,1:T(8,128)(2,1)S(1)}, bf16[384,24]{0,1:T(8,128)(2,1)S(1)}, u32[]{:S(2)}, u32[]{:S(2)}) collective-permute-start(bf16[384,24]{0,1:T(8,128)(2,1)S(1)} %get-tuple-element.152), channel_id=1, source_target_pairs={{0,16},{2,18},{4,20},{6,22},{8,24},{10,26},{12,28},{14,30},{16,0},... | collective-permute-start | bytes 55304 | tf_op jit(solution)/shard_map/ppermute | solution.py:30
  34.2 10.1 %collective-permute-start.8 = (bf16[384,24]{0,1:T(8,128)(2,1)S(1)}, bf16[384,24]{0,1:T(8,128)(2,1)S(1)}, u32[]{:S(2)}, u32[]{:S(2)}) collective-permute-start(bf16[384,24]{0,1:T(8,128)(2,1)S(1)} %get-tuple-element.151), channel_id=1, source_target_pairs={{0,18},{2,16},{4,22},{6,20},{8,26},{10,24},{12,30},{14,28},{16,2},... | collective-permute-start | bytes 55304 | tf_op jit(solution)/shard_map/ppermute | solution.py:30
  36.9 8.0 %collective-permute-start.9 = (bf16[384,24]{0,1:T(8,128)(2,1)S(1)}, bf16[384,24]{0,1:T(8,128)(2,1)S(1)}, u32[]{:S(2)}, u32[]{:S(2)}) collective-permute-start(bf16[384,24]{0,1:T(8,128)(2,1)S(1)} %get-tuple-element.150), channel_id=1, source_target_pairs={{0,20},{2,22},{4,16},{6,18},{8,28},{10,30},{12,24},{14,26},{16,4},... | collective-permute-start | bytes 55304 | tf_op jit(solution)/shard_map/ppermute | solution.py:30
  37.5 10.7 %collective-permute-start.10 = (bf16[384,24]{0,1:T(8,128)(2,1)S(1)}, bf16[384,24]{0,1:T(8,128)(2,1)S(1)}, u32[]{:S(2)}, u32[]{:S(2)}) collective-permute-start(bf16[384,24]{0,1:T(8,128)(2,1)S(1)} %get-tuple-element.149), channel_id=1, source_target_pairs={{0,22},{2,20},{4,18},{6,16},{8,30},{10,28},{12,26},{14,24},{16,6},... | collective-permute-start | bytes 55304 | tf_op jit(solution)/shard_map/ppermute | solution.py:30
  40.0 8.3 %collective-permute-start.11 = (bf16[384,24]{0,1:T(8,128)(2,1)S(1)}, bf16[384,24]{0,1:T(8,128)(2,1)S(1)}, u32[]{:S(2)}, u32[]{:S(2)}) collective-permute-start(bf16[384,24]{0,1:T(8,128)(2,1)S(1)} %get-tuple-element.148), channel_id=1, source_target_pairs={{0,24},{2,26},{4,28},{6,30},{8,16},{10,18},{12,20},{14,22},{16,8},... | collective-permute-start | bytes 55304 | tf_op jit(solution)/shard_map/ppermute | solution.py:30
  40.7 7.6 %collective-permute-start.12 = (bf16[384,24]{0,1:T(8,128)(2,1)S(1)}, bf16[384,24]{0,1:T(8,128)(2,1)S(1)}, u32[]{:S(2)}, u32[]{:S(2)}) collective-permute-start(bf16[384,24]{0,1:T(8,128)(2,1)S(1)} %get-tuple-element.147), channel_id=1, source_target_pairs={{0,26},{2,24},{4,30},{6,28},{8,18},{10,16},{12,22},{14,20},{16,10}... | collective-permute-start | bytes 55304 | tf_op jit(solution)/shard_map/ppermute | solution.py:30
  44.3 6.6 %collective-permute-start.13 = (bf16[384,24]{0,1:T(8,128)(2,1)S(1)}, bf16[384,24]{0,1:T(8,128)(2,1)S(1)}, u32[]{:S(2)}, u32[]{:S(2)}) collective-permute-start(bf16[384,24]{0,1:T(8,128)(2,1)S(1)} %get-tuple-element.146), channel_id=1, source_target_pairs={{0,28},{2,30},{4,24},{6,26},{8,20},{10,22},{12,16},{14,18},{16,12}... | collective-permute-start | bytes 55304 | tf_op jit(solution)/shard_map/ppermute | solution.py:30
  44.9 6.1 %collective-permute-start.14 = (bf16[384,24]{0,1:T(8,128)(2,1)S(1)}, bf16[384,24]{0,1:T(8,128)(2,1)S(1)}, u32[]{:S(2)}, u32[]{:S(2)}) collective-permute-start(bf16[384,24]{0,1:T(8,128)(2,1)S(1)} %get-tuple-element.145), channel_id=1, source_target_pairs={{0,30},{2,28},{4,26},{6,24},{8,22},{10,20},{12,18},{14,16},{16,14}... | collective-permute-start | bytes 55304 | tf_op jit(solution)/shard_map/ppermute | solution.py:30
  78.7 95.4 %copy-start = (f32[384,256]{1,0:T(8,128)S(1)}, f32[384,256]{1,0:T(8,128)}, u32[]{:S(2)}) copy-start(f32[384,256]{1,0:T(8,128)} %param.14) | copy-start | bytes 1179652
Sparse Core Ops, SparseCore 0:
  78.8 94.1 all-reduce.2
